TPU v7x, 32 devices: a whole 2x2x4 slice. The times are simulated.
32 devices in a mesh: ta: 4 (over z), ha: 2 (over y), wa: 4 (over x, core).
Axes of the slice: x: 2, y: 2, z: 4, core: 2. Of those that a mesh axis runs over, the one named last changes fastest.
Arguments:
- stream: bfloat16 [4, 2, 384, 1536], P('ta', 'ha'), may hold values from -40 to 40
- queries: bfloat16 [4, 2, 384, 1536], P('ta', 'ha', None, 'wa'), may hold values from -6 to 6
- key_heads: bfloat16 [4, 2, 384, 1536], P('ta', 'ha', None, 'wa'), may hold values from -6 to 6
- value_heads: bfloat16 [4, 2, 384, 1536], P('ta', 'ha', None, 'wa'), may hold values from -6 to 6
- out_weight: bfloat16 [1536, 1536], P('wa'), may hold values from -0.15625 to 0.15625
- norm_gain: float32 [1536], replicated, may hold values from 0.25 to 1.75
- up_weight: bfloat16 [1536, 6144], P(('ta', 'ha'), 'wa'), may hold values from -0.15625 to 0.15625
- down_weight: bfloat16 [6144, 1536], P('wa', ('ta', 'ha')), may hold values from -0.078125 to 0.078125
- tile_route: int32 [4, 2, 1], P('ta', 'ha'), may hold values 0 or 1
- cotangent: bfloat16 [4, 2, 384, 1536], P('ta', 'ha'), may hold values from -6 to 6
Outputs:
- stream_grad: bfloat16 [4, 2, 384, 1536], P('ta', 'ha')
- query_grad: bfloat16 [4, 2, 384, 1536], P('ta', 'ha', None, 'wa')
- key_grad: bfloat16 [4, 2, 384, 1536], P('ta', 'ha', None, 'wa')
- value_grad: bfloat16 [4, 2, 384, 1536], P('ta', 'ha', None, 'wa')
- out_weight_grad: float32 [1536, 1536], P('wa', ('ta', 'ha'))
All inputs are finite; a program needn't handle non-finite values. No bound on the sum of `tile_route` on one device may be relied on, other than what follows from the above.
Results may differ from a plain program's by a relative error of at most 0.014.
Values may be sent and summed in bfloat16 or wider, within the bound.
A program may use at most 128 MiB of HBM per device.

v0:
```python
import math
import jax
import jax.numpy as jnp
from jax import lax
from jax.sharding import PartitionSpec as P

HS = 128
TILE = 384
EPSILON = 1e-06
TANH_SCALE = 0.7978845608028654
CUBIC_COEF = 0.044715
NEG_FILL = -1e30


def extended(cells, sides, width):
    for axis, dim in sides:
        count = lax.axis_size(axis)
        ends = count - 1
        head = lax.slice_in_dim(cells, 0, width, axis=dim)
        tail = lax.slice_in_dim(cells, cells.shape[dim] - width, cells.shape[dim], axis=dim)
        cells = jnp.concatenate(
            [
                lax.ppermute(tail, axis, [(i, (i + 1) % count) for i in range(ends)]),
                cells,
                lax.ppermute(head, axis, [((i + 1) % count, i) for i in range(ends)]),
            ],
            axis=dim,
        )
    return cells


def from_behind(array, axis, by):
    devices = lax.axis_size(axis)
    pairs = [(i, i + by) for i in range(devices) if 0 <= i + by < devices]
    return lax.ppermute(array, axis, pairs)


def gelu_slope(pre_act):
    tanh_arg = TANH_SCALE * (pre_act + CUBIC_COEF * pre_act * pre_act * pre_act)
    tanh_val = jnp.tanh(tanh_arg)
    return 0.5 * (1.0 + tanh_val) + 0.5 * pre_act * (1.0 - tanh_val * tanh_val) * TANH_SCALE * (
        1.0 + 3.0 * CUBIC_COEF * pre_act * pre_act
    )


def head_probs(query_rows, key_rows, key_marks, score_scale):
    scores = (
        jnp.einsum("qd,kd->qk", query_rows, key_rows, preferred_element_type=jnp.float32)
        * score_scale
    )
    scores = jnp.where(key_marks[None, :] > 0.5, scores, NEG_FILL)
    row_max = jnp.max(scores, axis=1)
    weights = jnp.exp(scores - row_max[:, None])
    row_total = jnp.sum(weights, axis=1)
    return (weights / row_total[:, None], row_max, row_total)


def layer_norm(residual):
    mean_val = jnp.mean(residual, axis=1, keepdims=True)
    centered = residual - mean_val
    variance = jnp.mean(centered * centered, axis=1, keepdims=True)
    inv_std = lax.rsqrt(variance + EPSILON)
    return (centered * inv_std, inv_std)


def norm_backward(norm_grad, norm_gain, normed, inv_std):
    scaled = norm_grad * norm_gain
    return (
        scaled
        - jnp.mean(scaled, axis=1, keepdims=True)
        - normed * jnp.mean(scaled * normed, axis=1, keepdims=True)
    ) * inv_std


def shards(
    stream,
    queries,
    key_heads,
    value_heads,
    out_weight,
    norm_gain,
    up_weight,
    down_weight,
    tile_route,
    cotangent,
):
    row_count = stream.shape[2]
    model_width = stream.shape[3]
    channels = queries.shape[3]
    heads_here = channels // HS
    tile_count = row_count // TILE
    score_scale = 1.0 / math.sqrt(HS)
    tile_ids = jnp.arange(tile_count, dtype=jnp.int32)
    tile_marks = tile_route.astype(jnp.bfloat16)
    faces_key, faces_value, faces_marks = (
        extended(key_heads, (("ta", 0), ("ha", 1)), 1),
        extended(value_heads, (("ta", 0), ("ha", 1)), 1),
        extended(tile_marks, (("ta", 0), ("ha", 1)), 1),
    )

    def window():
        key_block = faces_key.reshape(9 * TILE, heads_here, HS)
        value_block = faces_value.reshape(9 * TILE, heads_here, HS)
        mark_block = faces_marks.reshape(9).astype(jnp.float32)
        key_marks = jnp.repeat(mark_block, TILE)
        query_tile = queries.reshape(TILE, heads_here, HS)
        return (
            query_tile.transpose(1, 0, 2),
            key_block.transpose(1, 0, 2),
            value_block.transpose(1, 0, 2),
            key_marks,
        )

    def forward_tile(tile_index):
        own_mark = tile_marks[0, 0, tile_index]
        query_tile, key_block, value_block, key_marks = window()

        def per_head(operands):
            query_rows, key_rows, value_rows = operands
            weights, row_max, row_total = head_probs(query_rows, key_rows, key_marks, score_scale)
            mixture = jnp.dot(
                weights.astype(jnp.bfloat16), value_rows, preferred_element_type=jnp.float32
            )
            return (mixture, row_max, row_total)

        mixture, row_max, row_total = lax.map(per_head, (query_tile, key_block, value_block))
        scaled = (mixture * own_mark.astype(jnp.float32)).astype(jnp.bfloat16)
        return (scaled.transpose(1, 0, 2).reshape(TILE, channels), row_max, row_total)

    attn_tiles, max_tiles, total_tiles = lax.map(forward_tile, tile_ids)
    attention = attn_tiles.reshape(row_count, channels)
    attn_part = jnp.dot(attention, out_weight, preferred_element_type=jnp.float32)
    head_share = lax.psum_scatter(attn_part, "wa", scatter_dimension=0, tiled=True)
    share_rows = head_share.shape[0]
    share_start = lax.axis_index("wa") * share_rows
    flat_stream = stream.reshape(row_count, model_width)
    flat_cot = cotangent.reshape(row_count, model_width)
    residual = (
        lax.dynamic_slice_in_dim(flat_stream, share_start, share_rows, 0).astype(jnp.float32)
        + head_share
    )
    normed, inv_std = layer_norm(residual)
    hidden_share = (normed * norm_gain).astype(jnp.bfloat16)
    hidden_in = lax.all_gather(hidden_share, "wa", axis=0, tiled=True)
    up_full, down_full = (
        lax.all_gather(up_weight, ("ta", "ha"), axis=0, tiled=True),
        lax.all_gather(down_weight, ("ta", "ha"), axis=1, tiled=True),
    )
    pre_act = jnp.dot(hidden_in, up_full, preferred_element_type=jnp.float32)
    act_grad = jnp.einsum("td,fd->tf", flat_cot, down_full, preferred_element_type=jnp.float32)
    pre_grad = (act_grad * gelu_slope(pre_act)).astype(jnp.bfloat16)
    norm_part = jnp.einsum("tf,df->td", pre_grad, up_full, preferred_element_type=jnp.float32)
    norm_share = lax.psum_scatter(norm_part, "wa", scatter_dimension=0, tiled=True)
    cot_share = lax.dynamic_slice_in_dim(flat_cot, share_start, share_rows, 0).astype(jnp.float32)
    grad_share = (cot_share + norm_backward(norm_share, norm_gain, normed, inv_std)).astype(
        jnp.bfloat16
    )
    stream_grad = lax.all_gather(grad_share, "wa", axis=0, tiled=True)
    weight_part = jnp.einsum(
        "tc,td->cd", attention, stream_grad, preferred_element_type=jnp.float32
    )
    out_weight_grad = lax.psum_scatter(weight_part, ("ta", "ha"), scatter_dimension=1, tiled=True)
    attn_grad = jnp.einsum(
        "td,cd->tc", stream_grad, out_weight, preferred_element_type=jnp.float32
    ).astype(jnp.bfloat16)
    row_marks = jnp.repeat(tile_marks.reshape(tile_count), TILE)
    masked_grad = attn_grad * row_marks[:, None]

    def own_side():
        query_tile, key_block, value_block, key_marks = window()
        grad_tile = masked_grad.reshape(TILE, heads_here, HS).transpose(1, 0, 2)

        def head_back(operands):
            query_rows, key_rows, value_rows, grad_rows = operands
            weights = head_probs(query_rows, key_rows, key_marks, score_scale)[0]
            grad_probs = jnp.einsum(
                "qd,kd->qk", grad_rows, value_rows, preferred_element_type=jnp.float32
            )
            row_delta = jnp.sum(weights * grad_probs, axis=1)
            grad_scores = (weights * (grad_probs - row_delta[:, None]) * score_scale).astype(
                jnp.bfloat16
            )
            query_part = jnp.dot(grad_scores, key_rows, preferred_element_type=jnp.float32).astype(
                jnp.bfloat16
            )
            value_part = jnp.einsum(
                "qk,qd->kd",
                weights.astype(jnp.bfloat16),
                grad_rows,
                preferred_element_type=jnp.float32,
            ).astype(jnp.bfloat16)
            key_part = jnp.einsum(
                "qk,qd->kd", grad_scores, query_rows, preferred_element_type=jnp.float32
            ).astype(jnp.bfloat16)
            return (query_part, row_delta, key_part, value_part)

        results = lax.map(head_back, (query_tile, key_block, value_block, grad_tile))
        query_part = results[0].transpose(1, 0, 2).reshape(TILE, channels)
        key_part = results[2].transpose(1, 0, 2).reshape(3, 3, TILE, channels)
        value_part = results[3].transpose(1, 0, 2).reshape(3, 3, TILE, channels)
        return (query_part, results[1], key_part, value_part)

    def guarded_own():
        blank_parts = (
            jnp.zeros((TILE, channels), jnp.bfloat16),
            jnp.zeros((heads_here, TILE), jnp.float32),
        )
        blank_parts = blank_parts + (
            jnp.zeros((3, 3, TILE, channels), jnp.bfloat16),
            jnp.zeros((3, 3, TILE, channels), jnp.bfloat16),
        )
        return own_side()

    def place_tile(carried, tile_index):
        query_part, row_delta, key_part, value_part = guarded_own()
        return ((key_part, value_part), query_part)

    empty_slots = jnp.zeros((3, 3, row_count, channels), jnp.bfloat16)
    (slots_key, slots_value), query_parts = lax.scan(
        place_tile, (empty_slots, empty_slots), tile_ids
    )
    middle_key = slots_key[1].astype(jnp.float32)
    middle_value = slots_value[1].astype(jnp.float32)
    for by_step, source in ((-1, 0), (1, 2)):
        moved_key, moved_value = from_behind(
            (slots_key[source], slots_value[source]), "ta", by_step
        )
        middle_key = middle_key + moved_key.astype(jnp.float32)
        middle_value = middle_value + moved_value.astype(jnp.float32)
    final_key = middle_key[1]
    final_value = middle_value[1]
    for by_step, source in ((-1, 0), (1, 2)):
        moved_key, moved_value = (
            from_behind(middle_key[source].astype(jnp.bfloat16), "ha", by_step).astype(jnp.float32),
            from_behind(middle_value[source].astype(jnp.bfloat16), "ha", by_step).astype(
                jnp.float32
            ),
        )
        final_key = final_key + moved_key
        final_value = final_value + moved_value
    key_grad = final_key.astype(jnp.bfloat16).reshape(1, 1, row_count, channels)
    value_grad = final_value.astype(jnp.bfloat16).reshape(1, 1, row_count, channels)
    query_grad = query_parts.reshape(1, 1, row_count, channels)
    return (
        stream_grad.reshape(1, 1, row_count, model_width),
        query_grad,
        key_grad,
        value_grad,
        out_weight_grad,
    )


def solution(mesh):
    placed = (
        P("ta", "ha", None, None),
        P("ta", "ha", None, "wa"),
        P("ta", "ha", None, "wa"),
        P("ta", "ha", None, "wa"),
        P("wa", None),
        P(),
        P(("ta", "ha"), "wa"),
        P("wa", ("ta", "ha")),
        P("ta", "ha", None),
        P("ta", "ha", None, None),
    )
    return jax.shard_map(
        shards,
        mesh=mesh,
        in_specs=placed,
        out_specs=(
            P("ta", "ha", None, None),
            P("ta", "ha", None, "wa"),
            P("ta", "ha", None, "wa"),
            P("ta", "ha", None, "wa"),
            P("wa", ("ta", "ha")),
        ),
        check_vma=False,
    )
```

profile of v0, /device:TPU:0, one launch (start us, length us, event | category | flops | bytes accessed | tf_op | source)
XLA Modules:
  0.0 548.8 jit_solution(6073854629250690570)
XLA Ops:
  30.7 6.4 %collective-permute-start.6 = (bf16[3,1,384,384]{3,2,1,0:T(8,128)(2,1)S(1)}, bf16[3,1,384,384]{3,2,1,0:T(8,128)(2,1)}, u32[]{:S(2)}, u32[]{:S(2)}) collective-permute-start(bf16[3,1,384,384]{3,2,1,0:T(8,128)(2,1)S(1)} %constant_dynamic-update-slice_fusion.1), channel_id=1, source_target_pairs={{0,4},{1,5},{2,6},{3,7},{8,12},{9,13},{10,14},{11,15},{16,20},{17,... | collective-permute-start | bytes 2654216 | tf_op jit(solution)/shard_map/ppermute | solution.py:23
  51.0 5.5 collective-permute-start.2
  56.6 6.5 %collective-permute-done.2 = bf16[3,1,1]{0,2,1:T(2,128)(2,1)S(1)} collective-permute-done((bf16[3,1,1]{0,2,1:T(2,128)(2,1)S(1)}, bf16[3,1,1]{0,2,1:T(2,128)(2,1)S(1)}, u32[]{:S(2)}, u32[]{:S(2)}) %collective-permute-start.2) | collective-permute-done | bytes 38 | tf_op jit(solution)/shard_map/ppermute | solution.py:23
  72.1 7.7 %reshape.147 = bf16[3456,3,128]{2,1,0:T(4,128)(2,1)} reshape(bf16[3,3,384,384]{3,2,1,0:T(8,128)(2,1)} %pad_maximum_fusion.1) | data formatting | bytes 5308416 | tf_op jit(solution)/shard_map/while/body/eval_jaxpr/reshape | solution.py:103
  87.0 7.7 %reshape.146 = bf16[3456,3,128]{2,1,0:T(4,128)(2,1)} reshape(bf16[3,3,384,384]{3,2,1,0:T(8,128)(2,1)} %pad_maximum_fusion) | data formatting | bytes 5308416 | tf_op jit(solution)/shard_map/while/body/eval_jaxpr/reshape | solution.py:102
  98.7 16.9 %while.44 = (s32[]{:T(128)}, f32[3,384,128]{1,2,0:T(8,128)S(1)}, bf16[3,384,128]{2,1,0:T(8,128)(2,1)S(1)}, bf16[3,3456,128]{2,1,0:T(8,128)(2,1)}, bf16[3,3456,128]{2,1,0:T(8,128)(2,1)}, /*index=5*/f32[9]{0:T(128)S(1)}, s32[]{:T(128)}) while((s32[]{:T(128)}, f32[3,384,128]{1,2,0:T(8,128)S(1)}, bf16[3,384,128]{2,1,0:T(8,128)(2,1)S(1)}, ...), condition=%wide.region_3.4_spmd.clone, body=%wide.region_0.3_spmd.clone.sunk | while | flops 690093312 | bytes 18014980 | solution.py:126
  118.0 32.4 %reduce-scatter.4.cloned.1.call-done = f32[96,1536]{1,0:T(8,128)} async-done(((f32[384,1536]{1,0:T(8,128)}), f32[96,1536]{1,0:T(8,128)}) %reduce-scatter.4.cloned.1.call-update) | async-done | bytes 589840 | tf_op jit(solution)/shard_map/reduce_scatter | solution.py:133
  154.7 15.8 %all-gather.7.cloned.1.call-done = bf16[384,1536]{1,0:T(8,128)(2,1)} async-done(((bf16[96,1536]{1,0:T(8,128)(2,1)}), bf16[384,1536]{1,0:T(8,128)(2,1)}) %all-gather.7.cloned.1.call-update) | async-done | bytes 1179664 | tf_op jit(solution)/shard_map/all_gather | solution.py:144
  170.5 82.3 %all-gather.9.cloned.1.call-done = bf16[1536,1536]{1,0:T(8,128)(2,1)} async-done(((bf16[192,1536]{1,0:T(8,128)(2,1)}), bf16[1536,1536]{1,0:T(8,128)(2,1)}) %all-gather.9.cloned.1.call-update) | async-done | bytes 4718608 | tf_op jit(solution)/shard_map/all_gather | solution.py:146
  252.8 6.1 %fusion.80 = f32[384,1536]{1,0:T(8,128)} fusion(bf16[384,1536]{1,0:T(8,128)(2,1)} %all-gather.7.cloned.1.call-done, bf16[1536,1536]{1,0:T(8,128)(2,1)} %all-gather.9.cloned.1.call-done), kind=kOutput, calls=%fused_computation.124 | convolution fusion | flops 1811939328 | bytes 8257536 | tf_op jit(solution)/shard_map/dot_general | solution.py:149
  258.9 74.3 %all-gather.5.cloned.1.call-done = bf16[1536,1536]{0,1:T(8,128)(2,1)} async-done(((bf16[1536,192]{0,1:T(8,128)(2,1)}), bf16[1536,1536]{0,1:T(8,128)(2,1)}) %all-gather.5.cloned.1.call-update) | async-done | bytes 4718608 | tf_op jit(solution)/shard_map/all_gather | solution.py:147
  333.1 10.0 %fusion.56 = f32[384,1536]{1,0:T(8,128)} fusion(bf16[1536,1536]{1,0:T(8,128)(2,1)} %all-gather.9.cloned.1.call-done, bf16[1536,1536]{0,1:T(8,128)(2,1)} %all-gather.5.cloned.1.call-done, f32[384,1536]{1,0:T(8,128)} %fusion.80, bf16[1,1,384,1536]{3,2,1,0:T(8,128)(2,1)} %param.23), kind=kOutput, calls=%fused_computation.75 | convolution fusion | flops 3635085312 | bytes 15335424 | tf_op jit(solution)/shard_map/tf,df->td/dot_general | solution.py:152
  343.3 31.3 %reduce-scatter.6.cloned.1.call-done = f32[96,1536]{1,0:T(8,128)} async-done(((f32[384,1536]{1,0:T(8,128)}), f32[96,1536]{1,0:T(8,128)}) %reduce-scatter.6.cloned.1.call-update) | async-done | bytes 589840 | tf_op jit(solution)/shard_map/reduce_scatter | solution.py:153
  378.2 17.5 %all-gather.11.cloned.1.call-done = bf16[384,1536]{1,0:T(8,128)(2,1)} async-done(((bf16[96,1536]{1,0:T(8,128)(2,1)}), bf16[384,1536]{1,0:T(8,128)(2,1)}) %all-gather.11.cloned.1.call-update) | async-done | bytes 1179664 | tf_op jit(solution)/shard_map/all_gather | solution.py:158
  400.5 43.7 %while.45 = (s32[]{:T(128)}, bf16[3,384,128]{1,2,0:T(8,128)(2,1)S(1)}, bf16[3,3456,128]{2,1,0:T(8,128)(2,1)}, bf16[3,3456,128]{2,1,0:T(8,128)(2,1)}, bf16[3,384,...) while((s32[]{:T(128)}, ...), condition=%wide.region_14.15_spmd.clone, body=%wide.region_10.14_spmd.clone.sunk | while | flops 1723513728 | bytes 71701848 | solution.py:197
  447.1 5.5 copy.58
  456.0 5.6 %copy.59 = bf16[1152,3,128]{2,1,0:T(4,128)(2,1)S(1)} copy(bf16[1152,3,128]{2,0,1:T(8,128)(2,1)} %get-tuple-element.257) | data formatting | bytes 1769472 | tf_op jit(solution)/shard_map/slice | solution.py:226
  463.6 5.5 collective-permute-start.17
  472.5 5.5 copy.55
  481.3 5.6 %copy.56 = bf16[1152,3,128]{2,1,0:T(4,128)(2,1)S(1)} copy(bf16[1152,3,128]{2,0,1:T(8,128)(2,1)} %get-tuple-element.260) | data formatting | bytes 1769472 | tf_op jit(solution)/shard_map/slice | solution.py:226
  488.9 5.7 %collective-permute-start.13 = (bf16[3,384,384]{2,1,0:T(8,128)(2,1)}, bf16[3,384,384]{2,1,0:T(8,128)(2,1)}, u32[]{:S(2)}, u32[]{:S(2)}) collective-permute-start(bf16[3,384,384]{2,1,0:T(8,128)(2,1)} %squeeze.56), channel_id=1, source_target_pairs={{0,8},{8,16},{16,24},{1,9},{9,17},{17,25},{2,10},{10,18},{18,26},{... | collective-permute-start | bytes 2654216 | tf_op jit(solution)/shard_map/ppermute | solution.py:35
  494.6 5.9 %copy.57 = f32[1152,3,128]{2,1,0:T(4,128)} copy(f32[1152,3,128]{2,0,1:T(8,128)S(1)} %get-tuple-element.258) | data formatting | bytes 3538944 | tf_op jit(solution)/shard_map/convert_element_type | solution.py:223
  504.8 5.9 %copy.54 = f32[1152,3,128]{2,1,0:T(4,128)} copy(f32[1152,3,128]{2,0,1:T(8,128)S(1)} %copy-done.2) | data formatting | bytes 3538944 | tf_op jit(solution)/shard_map/convert_element_type | solution.py:222
  529.5 5.3 collective-permute-start.15
  (182 shorter events, 179.1 us)
Async XLA Ops:
  7.2 143.2 %reduce-scatter.4.cloned.1.call-start = ((), (), s32[]{:S(2)}) async-start(), calls=%async_computation.4 | async-start | bytes 2949120 | tf_op jit(solution)/shard_map/reduce_scatter | solution.py:133
  7.2 12.6 %collective-permute-start.8 = (bf16[1,1,384,384]{3,2,1,0:T(8,128)(2,1)}, bf16[1,1,384,384]{3,2,1,0:T(8,128)(2,1)S(1)}, u32[]{:S(2)}, u32[]{:S(2)}) collective-permute-start(bf16[1,1,384,384]{3,2,1,0:T(8,128)(2,1)} %param.17), channel_id=1, source_target_pairs={{0,8},{8,16},{16,24},{1,9},{9,17},{17,25},{2,10},{10,18},{18,26},{... | collective-permute-start | bytes 884744 | tf_op jit(solution)/shard_map/ppermute | solution.py:23
  12.3 11.5 %collective-permute-start.9 = (bf16[1,1,384,384]{3,2,1,0:T(8,128)(2,1)}, bf16[1,1,384,384]{3,2,1,0:T(8,128)(2,1)S(1)}, u32[]{:S(2)}, u32[]{:S(2)}) collective-permute-start(bf16[1,1,384,384]{3,2,1,0:T(8,128)(2,1)} %param.17), channel_id=1, source_target_pairs={{8,0},{16,8},{24,16},{9,1},{17,9},{25,17},{10,2},{18,10},{26,18},{... | collective-permute-start | bytes 884744 | tf_op jit(solution)/shard_map/ppermute | solution.py:25
  13.6 15.9 %collective-permute-start.4 = (bf16[1,1,384,384]{3,2,1,0:T(8,128)(2,1)}, bf16[1,1,384,384]{3,2,1,0:T(8,128)(2,1)S(1)}, u32[]{:S(2)}, u32[]{:S(2)}) collective-permute-start(bf16[1,1,384,384]{3,2,1,0:T(8,128)(2,1)} %param.16), channel_id=1, source_target_pairs={{0,8},{8,16},{16,24},{1,9},{9,17},{17,25},{2,10},{10,18},{18,26},{... | collective-permute-start | bytes 884744 | tf_op jit(solution)/shard_map/ppermute | solution.py:23
  18.2 12.4 %collective-permute-start.5 = (bf16[1,1,384,384]{3,2,1,0:T(8,128)(2,1)}, bf16[1,1,384,384]{3,2,1,0:T(8,128)(2,1)S(1)}, u32[]{:S(2)}, u32[]{:S(2)}) collective-permute-start(bf16[1,1,384,384]{3,2,1,0:T(8,128)(2,1)} %param.16), channel_id=1, source_target_pairs={{8,0},{16,8},{24,16},{9,1},{17,9},{25,17},{10,2},{18,10},{26,18},{... | collective-permute-start | bytes 884744 | tf_op jit(solution)/shard_map/ppermute | solution.py:25
  23.9 44.9 %collective-permute-start.10 = (bf16[3,1,384,384]{3,2,1,0:T(8,128)(2,1)S(1)}, bf16[3,1,384,384]{3,2,1,0:T(8,128)(2,1)}, u32[]{:S(2)}, u32[]{:S(2)}) collective-permute-start(bf16[3,1,384,384]{3,2,1,0:T(8,128)(2,1)S(1)} %constant_dynamic-update-slice_fusion.4), channel_id=1, source_target_pairs={{0,4},{1,5},{2,6},{3,7},{8,12},{9,13},{10,14},{11,15},{16,20},{17,... | collective-permute-start | bytes 2654216 | tf_op jit(solution)/shard_map/ppermute | solution.py:23
  28.3 40.5 %collective-permute-start.11 = (bf16[3,1,384,384]{3,2,1,0:T(8,128)(2,1)S(1)}, bf16[3,1,384,384]{3,2,1,0:T(8,128)(2,1)}, u32[]{:S(2)}, u32[]{:S(2)}) collective-permute-start(bf16[3,1,384,384]{3,2,1,0:T(8,128)(2,1)S(1)} %constant_dynamic-update-slice_fusion.4), channel_id=1, source_target_pairs={{4,0},{5,1},{6,2},{7,3},{12,8},{13,9},{14,10},{15,11},{20,16},{21,... | collective-permute-start | bytes 2654216 | tf_op jit(solution)/shard_map/ppermute | solution.py:25
  30.7 53.0 %collective-permute-start.6 = (bf16[3,1,384,384]{3,2,1,0:T(8,128)(2,1)S(1)}, bf16[3,1,384,384]{3,2,1,0:T(8,128)(2,1)}, u32[]{:S(2)}, u32[]{:S(2)}) collective-permute-start(bf16[3,1,384,384]{3,2,1,0:T(8,128)(2,1)S(1)} %constant_dynamic-update-slice_fusion.1), channel_id=1, source_target_pairs={{0,4},{1,5},{2,6},{3,7},{8,12},{9,13},{10,14},{11,15},{16,20},{17,... | collective-permute-start | bytes 2654216 | tf_op jit(solution)/shard_map/ppermute | solution.py:23
  37.1 46.6 %collective-permute-start.7 = (bf16[3,1,384,384]{3,2,1,0:T(8,128)(2,1)S(1)}, bf16[3,1,384,384]{3,2,1,0:T(8,128)(2,1)}, u32[]{:S(2)}, u32[]{:S(2)}) collective-permute-start(bf16[3,1,384,384]{3,2,1,0:T(8,128)(2,1)S(1)} %constant_dynamic-update-slice_fusion.1), channel_id=1, source_target_pairs={{4,0},{5,1},{6,2},{7,3},{12,8},{13,9},{14,10},{15,11},{20,16},{21,... | collective-permute-start | bytes 2654216 | tf_op jit(solution)/shard_map/ppermute | solution.py:25
  51.0 12.1 %collective-permute-start.2 = (bf16[3,1,1]{0,2,1:T(2,128)(2,1)S(1)}, bf16[3,1,1]{0,2,1:T(2,128)(2,1)S(1)}, u32[]{:S(2)}, u32[]{:S(2)}) collective-permute-start(bf16[3,1,1]{0,2,1:T(2,128)(2,1)S(1)} %pad_maximum_fusion.2), channel_id=1, source_target_pairs={{0,4},{1,5},{2,6},{3,7},{8,12},{9,13},{10,14},{11,15},{16,20},{17,... | collective-permute-start | bytes 26 | tf_op jit(solution)/shard_map/ppermute | solution.py:23
  117.9 52.5 %all-gather.7.cloned.1.call-start = ((), (), s32[]{:S(2)}) async-start(), calls=%async_computation.5 | async-start | bytes 1474560 | tf_op jit(solution)/shard_map/all_gather | solution.py:144
  152.8 100.0 %all-gather.9.cloned.1.call-start = ((), (), s32[]{:S(2)}) async-start(), calls=%async_computation.6 | async-start | bytes 5308416 | tf_op jit(solution)/shard_map/all_gather | solution.py:146
  153.6 179.6 %all-gather.5.cloned.1.call-start = ((), (), s32[]{:S(2)}) async-start(), calls=%async_computation.3 | async-start | bytes 5308416 | tf_op jit(solution)/shard_map/all_gather | solution.py:147
  154.2 220.4 %reduce-scatter.6.cloned.1.call-start = ((), (), s32[]{:S(2)}) async-start(), calls=%async_computation.7 | async-start | bytes 2949120 | tf_op jit(solution)/shard_map/reduce_scatter | solution.py:153
  343.2 52.6 %all-gather.11.cloned.1.call-start = ((), (), s32[]{:S(2)}) async-start(), calls=%async_computation.8 | async-start | bytes 1474560 | tf_op jit(solution)/shard_map/all_gather | solution.py:158
  378.1 162.6 %reduce-scatter.8.cloned.1.call-start = ((), (), s32[]{:S(2)}) async-start(), calls=%async_computation.9 | async-start | bytes 2654208 | tf_op jit(solution)/shard_map/reduce_scatter | solution.py:162
  454.6 59.0 %collective-permute-start.16 = (bf16[3,384,384]{2,1,0:T(8,128)(2,1)}, bf16[3,384,384]{2,1,0:T(8,128)(2,1)}, u32[]{:S(2)}, u32[]{:S(2)}) collective-permute-start(bf16[3,384,384]{2,1,0:T(8,128)(2,1)} %squeeze.58), channel_id=1, source_target_pairs={{8,0},{16,8},{24,16},{9,1},{17,9},{25,17},{10,2},{18,10},{26,18},{... | collective-permute-start | bytes 2654216 | tf_op jit(solution)/shard_map/ppermute | solution.py:35
  463.6 50.0 %collective-permute-start.17 = (bf16[3,384,384]{2,1,0:T(8,128)(2,1)}, bf16[3,384,384]{2,1,0:T(8,128)(2,1)}, u32[]{:S(2)}, u32[]{:S(2)}) collective-permute-start(bf16[3,384,384]{2,1,0:T(8,128)(2,1)} %squeeze.59), channel_id=1, source_target_pairs={{0,8},{8,16},{16,24},{1,9},{9,17},{17,25},{2,10},{10,18},{18,26},{... | collective-permute-start | bytes 2654216 | tf_op jit(solution)/shard_map/ppermute | solution.py:35
  480.0 44.5 %collective-permute-start.12 = (bf16[3,384,384]{2,1,0:T(8,128)(2,1)}, bf16[3,384,384]{2,1,0:T(8,128)(2,1)}, u32[]{:S(2)}, u32[]{:S(2)}) collective-permute-start(bf16[3,384,384]{2,1,0:T(8,128)(2,1)} %squeeze.55), channel_id=1, source_target_pairs={{8,0},{16,8},{24,16},{9,1},{17,9},{25,17},{10,2},{18,10},{26,18},{... | collective-permute-start | bytes 2654216 | tf_op jit(solution)/shard_map/ppermute | solution.py:35
  488.9 35.6 %collective-permute-start.13 = (bf16[3,384,384]{2,1,0:T(8,128)(2,1)}, bf16[3,384,384]{2,1,0:T(8,128)(2,1)}, u32[]{:S(2)}, u32[]{:S(2)}) collective-permute-start(bf16[3,384,384]{2,1,0:T(8,128)(2,1)} %squeeze.56), channel_id=1, source_target_pairs={{0,8},{8,16},{16,24},{1,9},{9,17},{17,25},{2,10},{10,18},{18,26},{... | collective-permute-start | bytes 2654216 | tf_op jit(solution)/shard_map/ppermute | solution.py:35
  517.9 17.8 %collective-permute-start.18 = (bf16[384,384]{1,0:T(8,128)(2,1)}, bf16[384,384]{1,0:T(8,128)(2,1)S(1)}, u32[]{:S(2)}, u32[]{:S(2)}) collective-permute-start(bf16[384,384]{1,0:T(8,128)(2,1)} %get-tuple-element.262), channel_id=1, source_target_pairs={{4,0},{5,1},{6,2},{7,3},{12,8},{13,9},{14,10},{15,11},{20,16},{21,... | collective-permute-start | bytes 884744 | tf_op jit(solution)/shard_map/ppermute | solution.py:35
  519.2 16.5 %collective-permute-start.19 = (bf16[384,384]{1,0:T(8,128)(2,1)S(1)}, bf16[384,384]{1,0:T(8,128)(2,1)}, u32[]{:S(2)}, u32[]{:S(2)}) collective-permute-start(bf16[384,384]{1,0:T(8,128)(2,1)S(1)} %get-tuple-element.263), channel_id=1, source_target_pairs={{0,4},{1,5},{2,6},{3,7},{8,12},{9,13},{10,14},{11,15},{16,20},{17,... | collective-permute-start | bytes 884744 | tf_op jit(solution)/shard_map/ppermute | solution.py:35
  528.2 9.5 %collective-permute-start.14 = (bf16[384,384]{1,0:T(8,128)(2,1)}, bf16[384,384]{1,0:T(8,128)(2,1)S(1)}, u32[]{:S(2)}, u32[]{:S(2)}) collective-permute-start(bf16[384,384]{1,0:T(8,128)(2,1)} %get-tuple-element.264), channel_id=1, source_target_pairs={{4,0},{5,1},{6,2},{7,3},{12,8},{13,9},{14,10},{15,11},{20,16},{21,... | collective-permute-start | bytes 884744 | tf_op jit(solution)/shard_map/ppermute | solution.py:35
  529.5 9.2 %collective-permute-start.15 = (bf16[384,384]{1,0:T(8,128)(2,1)S(1)}, bf16[384,384]{1,0:T(8,128)(2,1)}, u32[]{:S(2)}, u32[]{:S(2)}) collective-permute-start(bf16[384,384]{1,0:T(8,128)(2,1)S(1)} %get-tuple-element.265), channel_id=1, source_target_pairs={{0,4},{1,5},{2,6},{3,7},{8,12},{9,13},{10,14},{11,15},{16,20},{17,... | collective-permute-start | bytes 884744 | tf_op jit(solution)/shard_map/ppermute | solution.py:35
  (17 other events, 235.4 us)
Sparse Core Ops, SparseCore 0:
  118.1 32.2 reduce-scatter.3
  153.0 17.4 all-gather.6
  172.9 79.8 all-gather.8
  255.1 78.0 all-gather.4
  343.3 31.1 reduce-scatter.5
  378.3 17.4 all-gather.10
  400.6 72.8 reduce-scatter.7
where the time goes:
time: 557 us; the launch traced here: 549 us
  waiting for transfers between devices  274 us (49%)
  local copies, waits for them, and re-layouts  84.7 us (15%)
  matrix products  66.8 us (12%)
  starting transfers between devices  66.1 us (12%)
  other arithmetic  41.6 us (7%)
  between operations  15.4 us (3%)
    all_gather x1, waiting for transfers between devices, shards(): lax.all_gather(up_weight, ('ta', 'ha'), axis=0, tiled=True)  82.3 us
    all_gather x1, waiting for transfers between devices, shards(): lax.all_gather(down_weight, ('ta', 'ha'), axis=1, tiled=True)  74.3 us
    reduce_scatter x1, waiting for transfers between devices, shards(): lax.psum_scatter(attn_part, 'wa', scatter_dimension=0, tiled=True)  32.4 us
    reduce_scatter x1, waiting for transfers between devices, shards(): lax.psum_scatter(norm_part, 'wa', scatter_dimension=0, tiled=True)  31.3 us
    ppermute x6, starting transfers between devices, extended(): lax.ppermute(tail, axis, [(i, (i + 1) % count) for i in range(ends)])  30.7 us
    ppermute x8, starting transfers between devices, from_behind(): return lax.ppermute(array, axis, pairs)  27 us
    all_gather x1, waiting for transfers between devices, shards(): stream_grad = lax.all_gather(grad_share, 'wa', axis=0, tiled=True)  17.5 us
    all_gather x1, waiting for transfers between devices, shards(): hidden_in = lax.all_gather(hidden_share, 'wa', axis=0, tiled=True)  15.8 us
  transfers between devices with their start and end apart: 27, of which 12 were waited for; matrix products, arithmetic and copies ran while one was open for 24% of the time, Pallas kernels for 0%

commit v1 on v0

--- a/solution.py
+++ b/solution.py
@@ -141,7 +141,12 @@
     )
     normed, inv_std = layer_norm(residual)
     hidden_share = (normed * norm_gain).astype(jnp.bfloat16)
-    hidden_in = lax.all_gather(hidden_share, "wa", axis=0, tiled=True)
+    ring = [hidden_share]
+    for hop in range(3):
+        ring.append(lax.ppermute(ring[-1], "wa", [(dev, (dev + 1) % 4) for dev in range(4)]))
+    hidden_in = jnp.roll(
+        jnp.concatenate(ring[::-1], axis=0), (lax.axis_index("wa") + 1) * ring[0].shape[0], axis=0
+    )
     up_full, down_full = (
         lax.all_gather(up_weight, ("ta", "ha"), axis=0, tiled=True),
         lax.all_gather(down_weight, ("ta", "ha"), axis=1, tiled=True),

time: 557 us -> 505 us (0.907)
  waiting for transfers between devices: 274 us -> 215 us
    all_gather x1, waiting for transfers between devices: 82.3 us -> 22.4 us  [shards(): lax.all_gather(up_weight, ('ta', 'ha'), axis=0, tiled=True)]
    ppermute x0 -> x3, waiting for transfers between devices: none -> 18.4 us  [shards(): lax.ppermute(ring[-1], 'wa', [(dev, (dev + 1) % 4) for dev in range(4)])]
    all_gather x1 -> x0, waiting for transfers between devices: 15.8 us -> none  [shards(): hidden_in = lax.all_gather(hidden_share, 'wa', axis=0, tiled=True)]
    unnamed x26 -> x32, local copies, waits for them, and re-layouts: 12.3 us -> 16.6 us
  transfers between devices with their start and end apart: 27 -> 29, of which waited for: 12 -> 14; matrix products, arithmetic and copies ran while one was open for 24% -> 28% of each run, Pallas kernels for 0% -> 0%
where the time goes in v1:
time: 505 us; the launch traced here: 497 us
  waiting for transfers between devices  215 us (43%)
  local copies, waits for them, and re-layouts  89.1 us (18%)
  matrix products  66.7 us (13%)
  starting transfers between devices  66.1 us (13%)
  other arithmetic  42.7 us (8%)
  between operations  16.8 us (3%)
    all_gather x1, waiting for transfers between devices, shards(): lax.all_gather(down_weight, ('ta', 'ha'), axis=1, tiled=True)  74 us
    reduce_scatter x1, waiting for transfers between devices, shards(): lax.psum_scatter(norm_part, 'wa', scatter_dimension=0, tiled=True)  31.4 us
    reduce_scatter x1, waiting for transfers between devices, shards(): lax.psum_scatter(attn_part, 'wa', scatter_dimension=0, tiled=True)  31.3 us
    ppermute x6, starting transfers between devices, extended(): lax.ppermute(tail, axis, [(i, (i + 1) % count) for i in range(ends)])  30.7 us
    ppermute x8, starting transfers between devices, from_behind(): return lax.ppermute(array, axis, pairs)  27 us
    all_gather x1, waiting for transfers between devices, shards(): lax.all_gather(up_weight, ('ta', 'ha'), axis=0, tiled=True)  22.4 us
    ppermute x3, waiting for transfers between devices, shards(): lax.ppermute(ring[-1], 'wa', [(dev, (dev + 1) % 4) for dev in range(4)])  18.4 us
    all_gather x1, waiting for transfers between devices, shards(): stream_grad = lax.all_gather(grad_share, 'wa', axis=0, tiled=True)  17.6 us
  transfers between devices with their start and end apart: 29, of which 14 were waited for; matrix products, arithmetic and copies ran while one was open for 28% of the time, Pallas kernels for 0%

profile of v1, /device:TPU:0, one launch (start us, length us, event | category | flops | bytes accessed | tf_op | source)
XLA Modules:
  0.0 496.8 jit_solution(10577667394080214062)
XLA Ops:
  31.5 6.4 %collective-permute-start.6 = (bf16[3,1,384,384]{3,2,1,0:T(8,128)(2,1)S(1)}, bf16[3,1,384,384]{3,2,1,0:T(8,128)(2,1)}, u32[]{:S(2)}, u32[]{:S(2)}) collective-permute-start(bf16[3,1,384,384]{3,2,1,0:T(8,128)(2,1)S(1)} %constant_dynamic-update-slice_fusion.1), channel_id=1, source_target_pairs={{0,4},{1,5},{2,6},{3,7},{8,12},{9,13},{10,14},{11,15},{16,20},{17,... | collective-permute-start | bytes 2654216 | tf_op jit(solution)/shard_map/ppermute | solution.py:23
  57.4 6.5 %collective-permute-done.2 = bf16[3,1,1]{0,2,1:T(2,128)(2,1)S(1)} collective-permute-done((bf16[3,1,1]{0,2,1:T(2,128)(2,1)S(1)}, bf16[3,1,1]{0,2,1:T(2,128)(2,1)S(1)}, u32[]{:S(2)}, u32[]{:S(2)}) %collective-permute-start.2) | collective-permute-done | bytes 38 | tf_op jit(solution)/shard_map/ppermute | solution.py:23
  72.9 7.7 %reshape.147 = bf16[3456,3,128]{2,1,0:T(4,128)(2,1)} reshape(bf16[3,3,384,384]{3,2,1,0:T(8,128)(2,1)} %pad_maximum_fusion.1) | data formatting | bytes 5308416 | tf_op jit(solution)/shard_map/while/body/eval_jaxpr/reshape | solution.py:103
  87.8 7.7 %reshape.146 = bf16[3456,3,128]{2,1,0:T(4,128)(2,1)} reshape(bf16[3,3,384,384]{3,2,1,0:T(8,128)(2,1)} %pad_maximum_fusion) | data formatting | bytes 5308416 | tf_op jit(solution)/shard_map/while/body/eval_jaxpr/reshape | solution.py:102
  99.5 16.9 %while.44 = (s32[]{:T(128)}, f32[3,384,128]{1,2,0:T(8,128)S(1)}, bf16[3,384,128]{2,1,0:T(8,128)(2,1)S(1)}, bf16[3,3456,128]{2,1,0:T(8,128)(2,1)}, bf16[3,3456,128]{2,1,0:T(8,128)(2,1)}, /*index=5*/f32[9]{0:T(128)S(1)}, s32[]{:T(128)}) while((s32[]{:T(128)}, f32[3,384,128]{1,2,0:T(8,128)S(1)}, bf16[3,384,128]{2,1,0:T(8,128)(2,1)S(1)}, ...), condition=%wide.region_3.4_spmd.clone, body=%wide.region_0.3_spmd.clone.sunk | while | flops 690093312 | bytes 18014980 | solution.py:126
  119.9 31.3 %reduce-scatter.4.cloned.1.call-done = f32[96,1536]{1,0:T(8,128)} async-done(((f32[384,1536]{1,0:T(8,128)}), f32[96,1536]{1,0:T(8,128)}) %reduce-scatter.4.cloned.1.call-update) | async-done | bytes 589840 | tf_op jit(solution)/shard_map/reduce_scatter | solution.py:133
  153.0 6.1 %collective-permute-done.12 = bf16[96,1536]{1,0:T(8,128)(2,1)S(1)} collective-permute-done((bf16[96,1536]{1,0:T(8,128)(2,1)S(1)}, bf16[96,1536]{1,0:T(8,128)(2,1)S(1)}, u32[]{:S(2)}, u32[]{:S(2)}) %collective-permute-start.12) | collective-permute-done | bytes 294944 | tf_op jit(solution)/shard_map/ppermute | solution.py:146
  159.2 6.1 %collective-permute-done.13 = bf16[96,1536]{1,0:T(8,128)(2,1)S(1)} collective-permute-done((bf16[96,1536]{1,0:T(8,128)(2,1)S(1)}, bf16[96,1536]{1,0:T(8,128)(2,1)S(1)}, u32[]{:S(2)}, u32[]{:S(2)}) %collective-permute-start.13) | collective-permute-done | bytes 294944 | tf_op jit(solution)/shard_map/ppermute | solution.py:146
  165.8 6.1 %collective-permute-done.14 = bf16[96,1536]{1,0:T(8,128)(2,1)S(1)} collective-permute-done((bf16[96,1536]{1,0:T(8,128)(2,1)S(1)}, bf16[96,1536]{1,0:T(8,128)(2,1)S(1)}, u32[]{:S(2)}, u32[]{:S(2)}) %collective-permute-start.14) | collective-permute-done | bytes 294944 | tf_op jit(solution)/shard_map/ppermute | solution.py:146
  178.0 22.4 %all-gather.6.cloned.1.call-done = bf16[1536,1536]{1,0:T(8,128)(2,1)} async-done(((bf16[192,1536]{1,0:T(8,128)(2,1)}), bf16[1536,1536]{1,0:T(8,128)(2,1)}) %all-gather.6.cloned.1.call-update) | async-done | bytes 4718608 | tf_op jit(solution)/shard_map/all_gather | solution.py:151
  200.4 6.1 %fusion.54 = f32[384,1536]{1,0:T(8,128)} fusion(bf16[1536,1536]{1,0:T(8,128)(2,1)} %all-gather.6.cloned.1.call-done, bf16[768,1536]{1,0:T(8,128)(2,1)} %constant_dynamic-update-slice_fusion.7, s32[]{:T(128)S(6)} %select_n.28), kind=kOutput, calls=%fused_computation.72 | convolution fusion | flops 1811939328 | bytes 8257540 | tf_op jit(solution)/shard_map/dot_general | solution.py:154
  206.4 74.0 %all-gather.4.cloned.1.call-done = bf16[1536,1536]{0,1:T(8,128)(2,1)} async-done(((bf16[1536,192]{0,1:T(8,128)(2,1)}), bf16[1536,1536]{0,1:T(8,128)(2,1)}) %all-gather.4.cloned.1.call-update) | async-done | bytes 4718608 | tf_op jit(solution)/shard_map/all_gather | solution.py:152
  280.4 10.0 %fusion.58 = f32[384,1536]{1,0:T(8,128)} fusion(bf16[1536,1536]{1,0:T(8,128)(2,1)} %all-gather.6.cloned.1.call-done, bf16[1536,1536]{0,1:T(8,128)(2,1)} %all-gather.4.cloned.1.call-done, f32[384,1536]{1,0:T(8,128)} %fusion.54, bf16[1,1,384,1536]{3,2,1,0:T(8,128)(2,1)} %param.23), kind=kOutput, calls=%fused_computation.77 | convolution fusion | flops 3635085312 | bytes 15335424 | tf_op jit(solution)/shard_map/tf,df->td/dot_general | solution.py:157
  290.5 31.4 %reduce-scatter.6.cloned.1.call-done = f32[96,1536]{1,0:T(8,128)} async-done(((f32[384,1536]{1,0:T(8,128)}), f32[96,1536]{1,0:T(8,128)}) %reduce-scatter.6.cloned.1.call-update) | async-done | bytes 589840 | tf_op jit(solution)/shard_map/reduce_scatter | solution.py:158
  325.6 17.6 %all-gather.8.cloned.1.call-done = bf16[384,1536]{1,0:T(8,128)(2,1)} async-done(((bf16[96,1536]{1,0:T(8,128)(2,1)}), bf16[384,1536]{1,0:T(8,128)(2,1)}) %all-gather.8.cloned.1.call-update) | async-done | bytes 1179664 | tf_op jit(solution)/shard_map/all_gather | solution.py:163
  347.9 43.7 %while.45 = (s32[]{:T(128)}, bf16[3,384,128]{1,2,0:T(8,128)(2,1)S(1)}, bf16[3,3456,128]{2,1,0:T(8,128)(2,1)}, bf16[3,3456,128]{2,1,0:T(8,128)(2,1)}, bf16[3,384,...) while((s32[]{:T(128)}, ...), condition=%wide.region_14.15_spmd.clone, body=%wide.region_10.14_spmd.clone.sunk | while | flops 1723513728 | bytes 71701848 | solution.py:202
  394.5 5.5 %copy.58 = bf16[1152,3,128]{2,1,0:T(4,128)(2,1)S(1)} copy(bf16[1152,3,128]{2,0,1:T(8,128)(2,1)S(1)} %get-tuple-element.256) | data formatting | bytes 1769472 | tf_op jit(solution)/shard_map/slice | solution.py:231
  403.4 5.6 %copy.59 = bf16[1152,3,128]{2,1,0:T(4,128)(2,1)S(1)} copy(bf16[1152,3,128]{2,0,1:T(8,128)(2,1)} %get-tuple-element.257) | data formatting | bytes 1769472 | tf_op jit(solution)/shard_map/slice | solution.py:231
  411.0 5.5 %collective-permute-start.20 = (bf16[3,384,384]{2,1,0:T(8,128)(2,1)}, bf16[3,384,384]{2,1,0:T(8,128)(2,1)}, u32[]{:S(2)}, u32[]{:S(2)}) collective-permute-start(bf16[3,384,384]{2,1,0:T(8,128)(2,1)} %squeeze.59), channel_id=1, source_target_pairs={{0,8},{8,16},{16,24},{1,9},{9,17},{17,25},{2,10},{10,18},{18,26},{... | collective-permute-start | bytes 2654216 | tf_op jit(solution)/shard_map/ppermute | solution.py:35
  419.9 5.5 %copy.55 = bf16[1152,3,128]{2,1,0:T(4,128)(2,1)S(1)} copy(bf16[1152,3,128]{2,0,1:T(8,128)(2,1)S(1)} %get-tuple-element.259) | data formatting | bytes 1769472 | tf_op jit(solution)/shard_map/slice | solution.py:231
  428.7 5.6 %copy.56 = bf16[1152,3,128]{2,1,0:T(4,128)(2,1)S(1)} copy(bf16[1152,3,128]{2,0,1:T(8,128)(2,1)} %get-tuple-element.260) | data formatting | bytes 1769472 | tf_op jit(solution)/shard_map/slice | solution.py:231
  436.3 5.7 %collective-permute-start.16 = (bf16[3,384,384]{2,1,0:T(8,128)(2,1)}, bf16[3,384,384]{2,1,0:T(8,128)(2,1)}, u32[]{:S(2)}, u32[]{:S(2)}) collective-permute-start(bf16[3,384,384]{2,1,0:T(8,128)(2,1)} %squeeze.56), channel_id=1, source_target_pairs={{0,8},{8,16},{16,24},{1,9},{9,17},{17,25},{2,10},{10,18},{18,26},{... | collective-permute-start | bytes 2654216 | tf_op jit(solution)/shard_map/ppermute | solution.py:35
  441.9 5.9 %copy.57 = f32[1152,3,128]{2,1,0:T(4,128)} copy(f32[1152,3,128]{2,0,1:T(8,128)S(1)} %get-tuple-element.258) | data formatting | bytes 3538944 | tf_op jit(solution)/shard_map/convert_element_type | solution.py:228
  452.1 5.9 %copy.54 = f32[1152,3,128]{2,1,0:T(4,128)} copy(f32[1152,3,128]{2,0,1:T(8,128)S(1)} %copy-done.2) | data formatting | bytes 3538944 | tf_op jit(solution)/shard_map/convert_element_type | solution.py:227
  (193 shorter events, 195.0 us)
Async XLA Ops:
  8.0 143.2 %reduce-scatter.4.cloned.1.call-start = ((), (), s32[]{:S(2)}) async-start(), calls=%async_computation.4 | async-start | bytes 2949120 | tf_op jit(solution)/shard_map/reduce_scatter | solution.py:133
  8.1 12.6 %collective-permute-start.8 = (bf16[1,1,384,384]{3,2,1,0:T(8,128)(2,1)}, bf16[1,1,384,384]{3,2,1,0:T(8,128)(2,1)S(1)}, u32[]{:S(2)}, u32[]{:S(2)}) collective-permute-start(bf16[1,1,384,384]{3,2,1,0:T(8,128)(2,1)} %param.17), channel_id=1, source_target_pairs={{0,8},{8,16},{16,24},{1,9},{9,17},{17,25},{2,10},{10,18},{18,26},{... | collective-permute-start | bytes 884744 | tf_op jit(solution)/shard_map/ppermute | solution.py:23
  13.2 11.5 %collective-permute-start.9 = (bf16[1,1,384,384]{3,2,1,0:T(8,128)(2,1)}, bf16[1,1,384,384]{3,2,1,0:T(8,128)(2,1)S(1)}, u32[]{:S(2)}, u32[]{:S(2)}) collective-permute-start(bf16[1,1,384,384]{3,2,1,0:T(8,128)(2,1)} %param.17), channel_id=1, source_target_pairs={{8,0},{16,8},{24,16},{9,1},{17,9},{25,17},{10,2},{18,10},{26,18},{... | collective-permute-start | bytes 884744 | tf_op jit(solution)/shard_map/ppermute | solution.py:25
  14.5 15.9 %collective-permute-start.4 = (bf16[1,1,384,384]{3,2,1,0:T(8,128)(2,1)}, bf16[1,1,384,384]{3,2,1,0:T(8,128)(2,1)S(1)}, u32[]{:S(2)}, u32[]{:S(2)}) collective-permute-start(bf16[1,1,384,384]{3,2,1,0:T(8,128)(2,1)} %param.16), channel_id=1, source_target_pairs={{0,8},{8,16},{16,24},{1,9},{9,17},{17,25},{2,10},{10,18},{18,26},{... | collective-permute-start | bytes 884744 | tf_op jit(solution)/shard_map/ppermute | solution.py:23
  19.0 12.4 %collective-permute-start.5 = (bf16[1,1,384,384]{3,2,1,0:T(8,128)(2,1)}, bf16[1,1,384,384]{3,2,1,0:T(8,128)(2,1)S(1)}, u32[]{:S(2)}, u32[]{:S(2)}) collective-permute-start(bf16[1,1,384,384]{3,2,1,0:T(8,128)(2,1)} %param.16), channel_id=1, source_target_pairs={{8,0},{16,8},{24,16},{9,1},{17,9},{25,17},{10,2},{18,10},{26,18},{... | collective-permute-start | bytes 884744 | tf_op jit(solution)/shard_map/ppermute | solution.py:25
  24.7 44.9 %collective-permute-start.10 = (bf16[3,1,384,384]{3,2,1,0:T(8,128)(2,1)S(1)}, bf16[3,1,384,384]{3,2,1,0:T(8,128)(2,1)}, u32[]{:S(2)}, u32[]{:S(2)}) collective-permute-start(bf16[3,1,384,384]{3,2,1,0:T(8,128)(2,1)S(1)} %constant_dynamic-update-slice_fusion.4), channel_id=1, source_target_pairs={{0,4},{1,5},{2,6},{3,7},{8,12},{9,13},{10,14},{11,15},{16,20},{17,... | collective-permute-start | bytes 2654216 | tf_op jit(solution)/shard_map/ppermute | solution.py:23
  29.1 40.5 %collective-permute-start.11 = (bf16[3,1,384,384]{3,2,1,0:T(8,128)(2,1)S(1)}, bf16[3,1,384,384]{3,2,1,0:T(8,128)(2,1)}, u32[]{:S(2)}, u32[]{:S(2)}) collective-permute-start(bf16[3,1,384,384]{3,2,1,0:T(8,128)(2,1)S(1)} %constant_dynamic-update-slice_fusion.4), channel_id=1, source_target_pairs={{4,0},{5,1},{6,2},{7,3},{12,8},{13,9},{14,10},{15,11},{20,16},{21,... | collective-permute-start | bytes 2654216 | tf_op jit(solution)/shard_map/ppermute | solution.py:25
  31.5 53.0 %collective-permute-start.6 = (bf16[3,1,384,384]{3,2,1,0:T(8,128)(2,1)S(1)}, bf16[3,1,384,384]{3,2,1,0:T(8,128)(2,1)}, u32[]{:S(2)}, u32[]{:S(2)}) collective-permute-start(bf16[3,1,384,384]{3,2,1,0:T(8,128)(2,1)S(1)} %constant_dynamic-update-slice_fusion.1), channel_id=1, source_target_pairs={{0,4},{1,5},{2,6},{3,7},{8,12},{9,13},{10,14},{11,15},{16,20},{17,... | collective-permute-start | bytes 2654216 | tf_op jit(solution)/shard_map/ppermute | solution.py:23
  37.9 46.6 %collective-permute-start.7 = (bf16[3,1,384,384]{3,2,1,0:T(8,128)(2,1)S(1)}, bf16[3,1,384,384]{3,2,1,0:T(8,128)(2,1)}, u32[]{:S(2)}, u32[]{:S(2)}) collective-permute-start(bf16[3,1,384,384]{3,2,1,0:T(8,128)(2,1)S(1)} %constant_dynamic-update-slice_fusion.1), channel_id=1, source_target_pairs={{4,0},{5,1},{6,2},{7,3},{12,8},{13,9},{14,10},{15,11},{20,16},{21,... | collective-permute-start | bytes 2654216 | tf_op jit(solution)/shard_map/ppermute | solution.py:25
  51.9 12.1 %collective-permute-start.2 = (bf16[3,1,1]{0,2,1:T(2,128)(2,1)S(1)}, bf16[3,1,1]{0,2,1:T(2,128)(2,1)S(1)}, u32[]{:S(2)}, u32[]{:S(2)}) collective-permute-start(bf16[3,1,1]{0,2,1:T(2,128)(2,1)S(1)} %pad_maximum_fusion.2), channel_id=1, source_target_pairs={{0,4},{1,5},{2,6},{3,7},{8,12},{9,13},{10,14},{11,15},{16,20},{17,... | collective-permute-start | bytes 26 | tf_op jit(solution)/shard_map/ppermute | solution.py:23
  118.7 81.7 %all-gather.6.cloned.1.call-start = ((), (), s32[]{:S(2)}) async-start(), calls=%async_computation.5 | async-start | bytes 5308416 | tf_op jit(solution)/shard_map/all_gather | solution.py:151
  119.3 161.1 %all-gather.4.cloned.1.call-start = ((), (), s32[]{:S(2)}) async-start(), calls=%async_computation.3 | async-start | bytes 5308416 | tf_op jit(solution)/shard_map/all_gather | solution.py:152
  119.9 202.1 %reduce-scatter.6.cloned.1.call-start = ((), (), s32[]{:S(2)}) async-start(), calls=%async_computation.6 | async-start | bytes 2949120 | tf_op jit(solution)/shard_map/reduce_scatter | solution.py:158
  165.3 6.6 %collective-permute-start.14 = (bf16[96,1536]{1,0:T(8,128)(2,1)S(1)}, bf16[96,1536]{1,0:T(8,128)(2,1)S(1)}, u32[]{:S(2)}, u32[]{:S(2)}) collective-permute-start(bf16[96,1536]{1,0:T(8,128)(2,1)S(1)} %collective-permute-done.13), channel_id=1, source_target_pairs={{0,1},{1,2},{2,3},{3,0},{4,5},{5,6},{6,7},{7,4},{8,9},{9,10},{10,1... | collective-permute-start | bytes 884744 | tf_op jit(solution)/shard_map/ppermute | solution.py:146
  290.5 52.7 %all-gather.8.cloned.1.call-start = ((), (), s32[]{:S(2)}) async-start(), calls=%async_computation.7 | async-start | bytes 1474560 | tf_op jit(solution)/shard_map/all_gather | solution.py:163
  325.5 162.6 %reduce-scatter.8.cloned.1.call-start = ((), (), s32[]{:S(2)}) async-start(), calls=%async_computation.8 | async-start | bytes 2654208 | tf_op jit(solution)/shard_map/reduce_scatter | solution.py:167
  402.0 59.0 %collective-permute-start.19 = (bf16[3,384,384]{2,1,0:T(8,128)(2,1)}, bf16[3,384,384]{2,1,0:T(8,128)(2,1)}, u32[]{:S(2)}, u32[]{:S(2)}) collective-permute-start(bf16[3,384,384]{2,1,0:T(8,128)(2,1)} %squeeze.58), channel_id=1, source_target_pairs={{8,0},{16,8},{24,16},{9,1},{17,9},{25,17},{10,2},{18,10},{26,18},{... | collective-permute-start | bytes 2654216 | tf_op jit(solution)/shard_map/ppermute | solution.py:35
  411.0 50.0 %collective-permute-start.20 = (bf16[3,384,384]{2,1,0:T(8,128)(2,1)}, bf16[3,384,384]{2,1,0:T(8,128)(2,1)}, u32[]{:S(2)}, u32[]{:S(2)}) collective-permute-start(bf16[3,384,384]{2,1,0:T(8,128)(2,1)} %squeeze.59), channel_id=1, source_target_pairs={{0,8},{8,16},{16,24},{1,9},{9,17},{17,25},{2,10},{10,18},{18,26},{... | collective-permute-start | bytes 2654216 | tf_op jit(solution)/shard_map/ppermute | solution.py:35
  427.4 44.5 %collective-permute-start.15 = (bf16[3,384,384]{2,1,0:T(8,128)(2,1)}, bf16[3,384,384]{2,1,0:T(8,128)(2,1)}, u32[]{:S(2)}, u32[]{:S(2)}) collective-permute-start(bf16[3,384,384]{2,1,0:T(8,128)(2,1)} %squeeze.55), channel_id=1, source_target_pairs={{8,0},{16,8},{24,16},{9,1},{17,9},{25,17},{10,2},{18,10},{26,18},{... | collective-permute-start | bytes 2654216 | tf_op jit(solution)/shard_map/ppermute | solution.py:35
  436.3 35.6 %collective-permute-start.16 = (bf16[3,384,384]{2,1,0:T(8,128)(2,1)}, bf16[3,384,384]{2,1,0:T(8,128)(2,1)}, u32[]{:S(2)}, u32[]{:S(2)}) collective-permute-start(bf16[3,384,384]{2,1,0:T(8,128)(2,1)} %squeeze.56), channel_id=1, source_target_pairs={{0,8},{8,16},{16,24},{1,9},{9,17},{17,25},{2,10},{10,18},{18,26},{... | collective-permute-start | bytes 2654216 | tf_op jit(solution)/shard_map/ppermute | solution.py:35
  465.3 17.8 %collective-permute-start.21 = (bf16[384,384]{1,0:T(8,128)(2,1)}, bf16[384,384]{1,0:T(8,128)(2,1)S(1)}, u32[]{:S(2)}, u32[]{:S(2)}) collective-permute-start(bf16[384,384]{1,0:T(8,128)(2,1)} %get-tuple-element.262), channel_id=1, source_target_pairs={{4,0},{5,1},{6,2},{7,3},{12,8},{13,9},{14,10},{15,11},{20,16},{21,... | collective-permute-start | bytes 884744 | tf_op jit(solution)/shard_map/ppermute | solution.py:35
  466.6 16.5 %collective-permute-start.22 = (bf16[384,384]{1,0:T(8,128)(2,1)S(1)}, bf16[384,384]{1,0:T(8,128)(2,1)}, u32[]{:S(2)}, u32[]{:S(2)}) collective-permute-start(bf16[384,384]{1,0:T(8,128)(2,1)S(1)} %get-tuple-element.263), channel_id=1, source_target_pairs={{0,4},{1,5},{2,6},{3,7},{8,12},{9,13},{10,14},{11,15},{16,20},{17,... | collective-permute-start | bytes 884744 | tf_op jit(solution)/shard_map/ppermute | solution.py:35
  475.6 9.6 %collective-permute-start.17 = (bf16[384,384]{1,0:T(8,128)(2,1)}, bf16[384,384]{1,0:T(8,128)(2,1)S(1)}, u32[]{:S(2)}, u32[]{:S(2)}) collective-permute-start(bf16[384,384]{1,0:T(8,128)(2,1)} %get-tuple-element.264), channel_id=1, source_target_pairs={{4,0},{5,1},{6,2},{7,3},{12,8},{13,9},{14,10},{15,11},{20,16},{21,... | collective-permute-start | bytes 884744 | tf_op jit(solution)/shard_map/ppermute | solution.py:35
  476.9 9.3 %collective-permute-start.18 = (bf16[384,384]{1,0:T(8,128)(2,1)S(1)}, bf16[384,384]{1,0:T(8,128)(2,1)}, u32[]{:S(2)}, u32[]{:S(2)}) collective-permute-start(bf16[384,384]{1,0:T(8,128)(2,1)S(1)} %get-tuple-element.265), channel_id=1, source_target_pairs={{0,4},{1,5},{2,6},{3,7},{8,12},{9,13},{10,14},{11,15},{16,20},{17,... | collective-permute-start | bytes 884744 | tf_op jit(solution)/shard_map/ppermute | solution.py:35
  (19 other events, 247.9 us)
Sparse Core Ops, SparseCore 0:
  118.8 32.3 reduce-scatter.3
  290.6 31.2 reduce-scatter.5
  325.6 17.4 all-gather.7
Sparse Core Ops, SparseCore 1:
  121.6 78.7 all-gather.5
  202.7 77.7 all-gather.3
  348.0 72.7 reduce-scatter.7
